TPU v7x, 256 devices: a whole 4x4x8 slice. The times are simulated.
256 devices in a mesh: feat: 4 (over y), dom: 64 (over x, z, core).
Axes of the slice: x: 4, y: 4, z: 8, core: 2. Of those that a mesh axis runs over, the one named last changes fastest.
Arguments:
- feats: bfloat16 [32768, 128], P('dom', 'feat'), may hold values from -6 to 6
- tile_src: int32 [16384], P('dom'), may hold values from 0 to 3
- tile_dst: int32 [16384], P('dom'), may hold values from 0 to 255
- tile_val: bfloat16 [16384, 128, 128], P('dom'), may hold values from 0 to 0.125, as said below
- tile_count: int32 [64], P('dom'), may hold values from 64 to 256, as said below
- self_one: bfloat16 [128, 256], P('feat'), may hold values from -0.5 to 0.5
- neigh_one: bfloat16 [128, 256], P('feat'), may hold values from -0.5 to 0.5
- bias_one: float32 [256], P('feat'), may hold values from -3 to 3
- self_two: bfloat16 [256, 256], P('feat'), may hold values from -0.375 to 0.375
- neigh_two: bfloat16 [256, 256], P('feat'), may hold values from -0.375 to 0.375
- bias_two: float32 [256], P('feat'), may hold values from -3 to 3
Outputs:
- hidden_two: bfloat16 [32768, 256], P('dom', 'feat')
Inputs may be any that keep to these rules, and one draw needn't show every extreme that they name: `tile_count`: partitions hold differing numbers of live tiles; some partition has all 256 slots live in every draw. `tile_val`: most entries are zero.
All inputs are finite; a program needn't handle non-finite values.
Results may differ from a plain program's by a relative error of at most 0.0034.
Values sent between devices are 32-bit elements; how exact they have to be, the bound alone decides.
A program may use at most 128 MiB of HBM per device.

v0:
```python
import jax
import jax.numpy as jnp
from jax import lax
from jax.sharding import PartitionSpec as P

BLK = 128


def tile_messages(values, tile_val, tile_src):
    width = values.shape[1]
    blocked = values.reshape(-1, BLK, width)
    picked = blocked[tile_src]
    return jnp.einsum("tij,tjc->tic", tile_val, picked, preferred_element_type=jnp.float32)


def route_rows(messages, tile_dst, live, count):
    blocks = count // BLK
    wanted = lax.iota(jnp.int32, blocks)
    routing = ((tile_dst[None, :] == wanted[:, None]) & live[None, :]).astype(jnp.float32)
    term = jnp.einsum("bt,tic->bic", routing, messages, precision=lax.Precision.HIGHEST)
    return term.reshape(count, messages.shape[2])


def packing(width):
    return max(1, 128 // width)


def packed_term(messages, tile_dst, live, count):
    width = messages.shape[2]
    factor = packing(width)
    node_term = route_rows(messages, tile_dst, live, count * factor)
    return node_term.reshape(count, width * factor)


def on_device(
    feats,
    tile_src,
    tile_dst,
    tile_val,
    tile_count,
    self_one,
    neigh_one,
    bias_one,
    self_two,
    neigh_two,
    bias_two,
):
    highest = lax.Precision.HIGHEST
    node_rows = feats.shape[0]
    live = lax.iota(jnp.int32, tile_src.shape[0]) < tile_count[0]
    messages_one = tile_messages(feats, tile_val, tile_src)
    width_one = messages_one.shape[2]
    factor_one = packing(width_one)
    packed_one = lax.psum_scatter(
        packed_term(messages_one, tile_dst, live, node_rows // factor_one * lax.axis_size("dom")),
        "dom",
        scatter_dimension=0,
        tiled=True,
    )
    agg_one = packed_one.reshape(node_rows, width_one)
    partial_one = jnp.dot(feats, self_one, preferred_element_type=jnp.float32)
    partial_one = partial_one + jnp.dot(agg_one, neigh_one.astype(jnp.float32), precision=highest)
    share_cols = bias_one.shape[0]
    summed = lax.psum(partial_one, "feat")
    share_one = lax.dynamic_slice_in_dim(summed, lax.axis_index("feat") * share_cols, share_cols, 1)
    hidden_one = jnp.maximum(share_one + bias_one, 0.0).astype(jnp.bfloat16)
    messages_two = tile_messages(hidden_one, tile_val, tile_src)
    width_two = messages_two.shape[2]
    factor_two = packing(width_two)
    packed_two = lax.psum_scatter(
        packed_term(messages_two, tile_dst, live, node_rows // factor_two * lax.axis_size("dom")),
        "dom",
        scatter_dimension=0,
        tiled=True,
    )
    agg_two = packed_two.reshape(node_rows, width_two)
    partial_two = jnp.dot(hidden_one, self_two, preferred_element_type=jnp.float32)
    partial_two = partial_two + jnp.dot(agg_two, neigh_two.astype(jnp.float32), precision=highest)
    share_two = lax.psum_scatter(partial_two, "feat", scatter_dimension=1, tiled=True)
    return jnp.maximum(share_two + bias_two, 0.0).astype(jnp.bfloat16)


def solution(mesh):
    placed = (
        P("dom", "feat"),
        P("dom"),
        P("dom"),
        P("dom", None, None),
        P("dom"),
        P("feat", None),
        P("feat", None),
        P("feat"),
        P("feat", None),
        P("feat", None),
        P("feat"),
    )
    return jax.shard_map(
        on_device, mesh=mesh, in_specs=placed, out_specs=P("dom", "feat"), check_vma=False
    )
```

profile of v0, /device:TPU:2, one launch (start us, length us, event | category | flops | bytes accessed | tf_op | source)
XLA Modules:
  0.0 480.3 jit_solution(6751388556955921707)
XLA Ops:
  7.2 0.7 compare_select_fusion
  7.9 1.0 gather_fusion
  8.9 0.0 copy-start.6
  8.9 6.8 %convolution_bitcast_fusion.1 = f32[256,128,32]{1,2,0:T(8,128)S(1)} fusion(bf16[256,128,32]{1,2,0:T(8,128)(2,1)S(1)} %gather_fusion, bf16[256,128,128]{2,1,0:T(8,128)(2,1)} %param.14), kind=kOutput, calls=%fused_computation.7 | convolution fusion | flops 268435456 | bytes 14680064 | tf_op jit(solution)/shard_map/tij,tjc->tic/dot_general | solution.py:13
  15.7 6.7 %fusion.2 = f32[256,128,32]{1,0,2:T(8,128)} fusion(f32[256,128,32]{1,2,0:T(8,128)S(1)} %convolution_bitcast_fusion.1, s32[256]{0:T(256)S(1)} %copy-done.6, pred[256]{0:T(512)(128)(4,1)S(1)} %iota_compare_fusion.1), kind=kOutput, calls=%fused_computation.4 | convolution fusion | flops 3221356544 | bytes 8389888 | tf_op jit(solution)/shard_map/bt,tic->bic/dot_general | solution.py:20
  22.4 10.6 %copy.17 = f32[256,128,32]{2,1,0:T(8,128)} copy(f32[256,128,32]{1,0,2:T(8,128)} %fusion.2) | data formatting | bytes 8388608 | tf_op jit(solution)/shard_map/bt,tic->bic/dot_general | solution.py:20
  33.0 12.0 %reshape_reshape.6 = f32[8192,128]{1,0:T(8,128)} reshape(f32[256,128,32]{2,1,0:T(8,128)} %copy.17) | data formatting | bytes 8388608 | tf_op jit(solution)/shard_map/reshape;reshape | solution.py:32
  45.0 0.0 reduce-scatter.4.cloned.1.call-update
  45.0 0.0 all-reduce.2.cloned.1.call-start
  45.0 0.3 fusion.14
  45.3 145.7 %reduce-scatter.4.cloned.1.call-done = f32[128,128]{1,0:T(8,128)} async-done(((f32[8192,128]{1,0:T(8,128)}), f32[128,128]{1,0:T(8,128)}) %reduce-scatter.4.cloned.1.call-update) | async-done | bytes 65552 | tf_op jit(solution)/shard_map/reduce_scatter | solution.py:54
  191.0 0.9 reshape.20
  192.0 1.2 convolution_add_fusion.1
  193.2 0.0 all-reduce.2.cloned.1.call-update
  193.2 0.2 reduce-scatter.6.cloned.1.call-start
  193.5 47.4 %all-reduce.2.cloned.1.call-done = f32[512,256]{0,1:T(8,128)} async-done(((f32[512,256]{0,1:T(8,128)}), f32[512,256]{0,1:T(8,128)}) %all-reduce.2.cloned.1.call-update) | async-done | bytes 524304 | tf_op jit(solution)/shard_map/psum | solution.py:64
  240.9 1.0 copy_bitcast_fusion
  241.9 3.0 gather_fusion.1
  244.9 10.5 %convolution_bitcast_fusion = f32[256,128,64]{1,2,0:T(8,128)S(1)} fusion(bf16[256,128,64]{1,2,0:T(8,128)(2,1)} %gather_fusion.1, bf16[256,128,128]{2,1,0:T(8,128)(2,1)} %param.14), kind=kOutput, calls=%fused_computation.6 | convolution fusion | flops 536870912 | bytes 20971520 | tf_op jit(solution)/shard_map/tij,tjc->tic/dot_general | solution.py:13
  255.4 13.7 %fusion = f32[256,128,64]{1,0,2:T(8,128)} fusion(f32[256,128,64]{1,2,0:T(8,128)S(1)} %convolution_bitcast_fusion, s32[256]{0:T(256)S(1)} %copy-done.6, pred[256]{0:T(512)(128)(4,1)S(1)} %iota_compare_fusion.1), kind=kOutput, calls=%fused_computation.2 | convolution fusion | flops 6442582016 | bytes 16778496 | tf_op jit(solution)/shard_map/bt,tic->bic/dot_general | solution.py:20
  269.1 12.3 %copy.20 = f32[256,128,64]{2,1,0:T(8,128)} copy(f32[256,128,64]{1,0,2:T(8,128)} %fusion) | data formatting | bytes 16777216 | tf_op jit(solution)/shard_map/bt,tic->bic/dot_general | solution.py:20
  281.4 13.8 %reshape_reshape.7 = f32[16384,128]{1,0:T(8,128)} reshape(f32[256,128,64]{2,1,0:T(8,128)} %copy.20) | data formatting | bytes 16777216 | tf_op jit(solution)/shard_map/reshape;reshape | solution.py:32
  295.2 0.0 reduce-scatter.6.cloned.1.call-update
  295.2 0.0 reduce-scatter.8.cloned.1.call-start
  295.2 0.7 copy-done.2
  295.9 1.2 fusion.13
  297.1 149.6 %reduce-scatter.6.cloned.1.call-done = f32[256,128]{1,0:T(8,128)} async-done(((f32[16384,128]{1,0:T(8,128)}), f32[256,128]{1,0:T(8,128)}) %reduce-scatter.6.cloned.1.call-update) | async-done | bytes 131088 | tf_op jit(solution)/shard_map/reduce_scatter | solution.py:70
  446.7 1.0 reshape.22
  447.7 1.2 convolution_add_fusion
  448.9 0.0 reduce-scatter.8.cloned.1.call-update
  449.0 23.2 %reduce-scatter.8.cloned.1.call-done = f32[512,64]{0,1:T(8,128)} async-done(((f32[512,256]{0,1:T(8,128)}), f32[512,64]{0,1:T(8,128)}) %reduce-scatter.8.cloned.1.call-update) | async-done | bytes 131088 | tf_op jit(solution)/shard_map/reduce_scatter | solution.py:79
  472.2 1.6 maximum_convert_fusion
  (20 shorter events, 0.1 us)
Async XLA Ops:
  6.5 1.4 copy-start
  6.5 184.5 %reduce-scatter.4.cloned.1.call-start = ((), (), s32[]{:S(2)}) async-start(), calls=%async_computation.3 | async-start | bytes 4259840 | tf_op jit(solution)/shard_map/reduce_scatter | solution.py:54
  8.9 6.8 %copy-start.6 = (s32[256]{0:T(256)S(1)}, s32[256]{0:T(256)}, u32[]{:S(2)}) copy-start(s32[256]{0:T(256)} %param.13) | copy-start | bytes 3076
  32.9 12.1 %copy-start.4 = (bf16[32,256]{1,0:T(8,128)(2,1)S(1)}, bf16[32,256]{1,0:T(8,128)(2,1)}, u32[]{:S(2)}) copy-start(bf16[32,256]{1,0:T(8,128)(2,1)} %param.16) | copy-start | bytes 49156
  32.9 159.0 %copy-start.5 = (bf16[32,256]{1,0:T(8,128)(2,1)S(1)}, bf16[32,256]{1,0:T(8,128)(2,1)}, u32[]{:S(2)}) copy-start(bf16[32,256]{1,0:T(8,128)(2,1)} %param.17) | copy-start | bytes 49156
  32.9 207.9 %copy-start.7 = (f32[64]{0:T(128)S(1)}, f32[64]{0:T(128)}, u32[]{:S(2)}) copy-start(f32[64]{0:T(128)} %param.18) | copy-start | bytes 772
  45.0 195.9 %all-reduce.2.cloned.1.call-start = ((), (), s32[]{:S(2)}) async-start(), calls=%async_computation.4 | async-start | bytes 1048576 | tf_op jit(solution)/shard_map/psum | solution.py:64
  193.2 253.5 %reduce-scatter.6.cloned.1.call-start = ((), (), s32[]{:S(2)}) async-start(), calls=%async_computation.5 | async-start | bytes 8519680 | tf_op jit(solution)/shard_map/reduce_scatter | solution.py:70
  281.4 192.4 %copy-start.1 = (bf16[512,32]{0,1:T(8,128)(2,1)S(1)}, bf16[512,32]{0,1:T(8,128)(2,1)}, u32[]{:S(2)}) copy-start(bf16[512,32]{0,1:T(8,128)(2,1)} %param.11) | copy-start | bytes 98308
  295.2 0.8 copy-start.2
  295.2 152.6 %copy-start.3 = (bf16[64,256]{1,0:T(8,128)(2,1)S(1)}, bf16[64,256]{1,0:T(8,128)(2,1)}, u32[]{:S(2)}) copy-start(bf16[64,256]{1,0:T(8,128)(2,1)} %param.20) | copy-start | bytes 98308
  295.2 177.0 %copy-start.8 = (f32[64]{0:T(128)S(1)}, f32[64]{0:T(128)}, u32[]{:S(2)}) copy-start(f32[64]{0:T(128)} %param.21) | copy-start | bytes 772
  295.2 177.0 %reduce-scatter.8.cloned.1.call-start = ((), (), s32[]{:S(2)}) async-start(), calls=%async_computation.6 | async-start | bytes 655360 | tf_op jit(solution)/shard_map/reduce_scatter | solution.py:79
Sparse Core Ops, SparseCore 0:
  45.1 145.8 reduce-scatter.3
  193.5 47.3 all-reduce.1
  295.3 151.3 reduce-scatter.5
  449.1 23.0 reduce-scatter.7
where the time goes:
time: 482 us; the launch traced here: 480 us
  waiting for transfers between devices  366 us (76%)
  local copies, waits for them, and re-layouts  55.4 us (11%)
  matrix products  41.5 us (9%)
  between operations  13.9 us (3%)
    reduce_scatter x1, waiting for transfers between devices, on_device(): lax.psum_scatter(packed_term(messages_two, tile_dst, live, node_rows // f...  150 us
    reduce_scatter x1, waiting for transfers between devices, on_device(): lax.psum_scatter(packed_term(messages_one, tile_dst, live, node_rows // f...  146 us
    psum x1, waiting for transfers between devices, on_device(): summed = lax.psum(partial_one, 'feat')  47.4 us
    another operation x2, local copies, waits for them, and re-layouts, packed_term(): return node_term.reshape(count, width * factor)  25.8 us
    reduce_scatter x1, waiting for transfers between devices, on_device(): lax.psum_scatter(partial_two, 'feat', scatter_dimension=1, tiled=True)  23.2 us
    dot_general x2, local copies, waits for them, and re-layouts, route_rows(): jnp.einsum('bt,tic->bic', routing, messages, precision=lax.Precision.HIGH...  22.9 us
    dot_general x2, matrix products, route_rows(): jnp.einsum('bt,tic->bic', routing, messages, precision=lax.Precision.HIGH...  20.3 us
    dot_general x2, matrix products, tile_messages(): jnp.einsum('tij,tjc->tic', tile_val, picked, preferred_element_type=jnp.f...  17.3 us
  transfers between devices with their start and end apart: 4, of which 4 were waited for; matrix products, arithmetic and copies ran while one was open for 0% of the time, Pallas kernels for 0%

commit v1 on v0

v1 whole, which is shorter than its diff:
```python
import functools

import jax
import jax.numpy as jnp
from jax import lax
from jax.experimental import pallas as pl
from jax.experimental.pallas import tpu as pltpu
from jax.sharding import PartitionSpec as P

MESH = pl.DeviceIdType.MESH
BLK = 128
QUARTER = 32
XS, ZS, FS = 4, 8, 4
TILES = 256
GROUP = 32
PACK_ROWS = 200
F32, BF16 = jnp.float32, jnp.bfloat16


def position():
    dom = lax.axis_index("dom")
    return lax.div(dom, 2 * ZS), lax.rem(lax.div(dom, 2), ZS), lax.rem(dom, 2)


def rank_of(offset, middle):
    return 2 * (offset - middle) if offset >= middle else 2 * (middle - offset) - 1


def chunk_x(dx, half):
    return 2 * (2 * rank_of(dx, XS // 2) + half) + 1


def chunk_z(dz):
    return 2 * rank_of(dz, ZS // 2)


def traced_rank(offset, middle):
    ahead = offset - middle
    return jnp.where(ahead >= 0, 2 * ahead, -2 * ahead - 1)


def build_kernel(
    count_ref, src_ref, dst_ref, tiles_ref, feats_ref, self_one_ref, neigh_one_ref, bias_one_ref, self_two_ref,
    neigh_two_ref, bias_two_ref, adj, feats_out, pack_out,
    tiles, src, dst, feats, self_one, neigh_one, bias_one, self_two, neigh_two, bias_two, total, order, cells, earlier,
    last, in_sems, small_sems,
):
    def load(source, target, n):
        copy = pltpu.make_async_copy(source, target, small_sems.at[n])
        copy.start()
        return copy

    index_loads = [load(src_ref, src, 0), load(dst_ref, dst, 1)]
    loads = []
    groups = TILES // GROUP
    for g in range(groups):
        part = pl.ds(g * GROUP, GROUP)
        loads.append(pltpu.make_async_copy(tiles_ref.at[part], tiles.at[part], in_sems.at[g]))
        loads[-1].start()
    weight_loads = [
        load(feats_ref, feats, 2), load(self_one_ref, self_one, 3), load(neigh_one_ref, neigh_one, 4),
        load(bias_one_ref, bias_one, 5), load(self_two_ref, self_two, 6), load(neigh_two_ref, neigh_two, 7),
        load(bias_two_ref, bias_two, 8),
    ]
    feat = lax.axis_index("feat")
    x, z, core = position()
    count = count_ref[0]

    def clear(i, carry):
        adj[i] = jnp.zeros(adj.shape[1:], BF16)
        return carry

    lax.fori_loop(0, adj.shape[0], clear, 0)

    def forget(i, carry):
        last[i] = -1
        return carry

    lax.fori_loop(0, 256, forget, 0, unroll=16)
    for copy in index_loads:
        copy.wait()

    def look(t, hits):
        to = dst[t]
        dom = lax.shift_right_logical(to, 2)
        other = lax.bitwise_xor(dom & 1, core)
        dz = (lax.shift_right_logical(dom, 1) - z) & (ZS - 1)
        dx = (lax.shift_right_logical(dom, 4) - x) & (XS - 1)
        mine = jnp.logical_and((to & 3) == feat, t < count)
        cell = jnp.where(mine, ((other * XS + dx) * ZS + dz) * 4 + src[t], 256)
        earlier[t] = last[cell]
        last[cell] = t
        order[hits] = t
        cells[hits] = cell
        return hits + mine.astype(jnp.int32)

    ends = [jnp.int32(0)]
    for g in range(groups):
        ends.append(lax.fori_loop(g * GROUP, (g + 1) * GROUP, look, ends[-1], unroll=8))

    for copy in weight_loads:
        copy.wait()
    feats_out[...] = feats[...].astype(F32)
    pack_out[0:32, :] = self_one[...].astype(F32)
    pack_out[32:64, :] = neigh_one[...].astype(F32)
    pack_out[64:128, :] = self_two[...].astype(F32)
    pack_out[128:192, :] = neigh_two[...].astype(F32)
    pack_out[192:200, :] = jnp.zeros((8, 256), F32)
    pack_out[192:193, 0:64] = bias_one[...]
    pack_out[193:194, 0:64] = bias_two[...]

    def put(cell, value):
        source = cell & 3
        dz = lax.shift_right_logical(cell, 2) & (ZS - 1)
        dx = lax.shift_right_logical(cell, 5) & (XS - 1)
        base = lax.shift_right_logical(cell, 7) * 16
        lanes = pl.ds(pl.multiple_of(source * BLK, BLK), BLK)
        rank_x, rank_z = traced_rank(dx, XS // 2), traced_rank(dz, ZS // 2)
        for half in range(2):
            chunk = base + 2 * (2 * rank_x + half) + 1
            rows = pl.ds(pl.multiple_of(rank_z * QUARTER, QUARTER), QUARTER)
            adj[chunk, rows, lanes] = value[half * QUARTER : (half + 1) * QUARTER]
        chunk = base + 2 * rank_z
        for half in range(2):
            rows = pl.ds(pl.multiple_of(half * BLK + rank_x * QUARTER, QUARTER), QUARTER)
            adj[chunk, rows, lanes] = value[64 + half * QUARTER : 64 + (half + 1) * QUARTER]

    def fill(i, carry):
        t = order[i]
        cell = cells[i]
        before = earlier[t]

        @pl.when(last[cell] == t)
        def _():
            @pl.when(before < 0)
            def _():
                put(cell, tiles[t])

            @pl.when(before >= 0)
            def _():
                total[...] = tiles[t].astype(F32)

                def more(at):
                    total[...] += tiles[at].astype(F32)
                    return earlier[at]

                lax.while_loop(lambda at: at >= 0, more, before)
                put(cell, total[...].astype(BF16))

        return carry

    for g in range(groups):
        loads[g].wait()
        lax.fori_loop(ends[g], ends[g + 1], fill, 0)


def build(src, dst, count, tiles, feats, self_one, neigh_one, bias_one, self_two, neigh_two, bias_two):
    vmem = pl.BlockSpec(memory_space=pltpu.VMEM)
    hbm = pl.BlockSpec(memory_space=pltpu.HBM)
    arrays = [src, dst, tiles, feats, self_one, neigh_one, bias_one, self_two, neigh_two, bias_two]
    arrays = [pltpu.with_memory_space_constraint(array, pltpu.HBM) for array in arrays]
    smem = [pltpu.SMEM((TILES + 8,), jnp.int32)] * 3 + [pltpu.SMEM((264,), jnp.int32)]
    return pl.pallas_call(
        build_kernel,
        out_shape=(
            pltpu.VMEM((32, 256, 512), BF16),
            pltpu.VMEM((32, 512), F32),
            pltpu.VMEM((PACK_ROWS, 256), F32),
        ),
        in_specs=[pl.BlockSpec(memory_space=pltpu.SMEM)] + [hbm] * 10,
        out_specs=(vmem, vmem, vmem),
        scratch_shapes=[
            pltpu.VMEM((TILES, BLK, BLK), BF16),
            pltpu.SMEM((TILES,), jnp.int32),
            pltpu.SMEM((TILES,), jnp.int32),
        ]
        + [pltpu.VMEM(array.shape, array.dtype) for array in arrays[3:]]
        + [pltpu.VMEM((BLK, BLK), F32)]
        + smem
        + [pltpu.SemaphoreType.DMA((TILES // GROUP,)), pltpu.SemaphoreType.DMA((9,))],
        compiler_params=pltpu.CompilerParams(vmem_limit_bytes=12 << 20),
    )(count, *arrays)


def add_up(into, terms):
    rows = into.shape[0]
    step = rows if rows <= 160 else BLK

    def body(i, carry):
        part = pl.ds(pl.multiple_of(i * step, step), step)
        value = terms[0][part, :]
        for term in terms[1:]:
            value = value + term[part, :]
        into[part, :] = value
        return carry

    if rows == step:
        body(0, 0)
    else:
        lax.fori_loop(0, rows // step, body, 0)


class Ring:
    def __init__(self, n, own, extra, land, up_id, down_id, sends, recvs, started):
        self.n, self.middle = n, n // 2
        self.own, self.extra, self.land = own, extra, land
        self.ids = (up_id, down_id)
        self.sends, self.recvs, self.started = sends, recvs, started

    def copy(self, way, distance, half):
        offset = distance if way == 0 else self.n - distance
        slot = (way * self.middle + distance - 1) * 2 + half
        return pltpu.make_async_remote_copy(
            src_ref=self.own(offset, half),
            dst_ref=self.land(way, distance - 1, half),
            send_sem=self.sends.at[slot],
            recv_sem=self.recvs.at[slot],
            device_id=self.ids[way],
            device_id_type=MESH,
        )

    def gather_terms(self, way, distance, half):
        first = self.middle if way == half else self.middle - 1
        if distance == first:
            return []
        self.copy(way, distance + 1, half).wait_recv()
        return [self.land(way, distance, half)]

    def send(self, way, distance, half):
        offset = distance if way == 0 else self.n - distance
        mine = self.own(offset, half)
        terms = [mine] + self.extra(offset, half) + self.gather_terms(way, distance, half)
        if len(terms) > 1:
            add_up(mine, terms)
        copy = self.copy(way, distance, half)
        copy.start()
        self.started.append(copy)

    def early(self, distance):
        self.send(0, distance, 1)
        self.send(1, distance, 0)

    def late(self, distance):
        self.send(0, distance, 0)
        self.send(1, distance, 1)

    def finish(self, half, into=None):
        mine = self.own(0, half)
        terms = [mine] + self.extra(0, half)
        for way in range(2):
            terms += self.gather_terms(way, 0, half)
        add_up(mine if into is None else into, terms)


def split(value):
    high = value.astype(BF16)
    rest = value - high.astype(F32)
    middle = rest.astype(BF16)
    low = (rest - middle.astype(F32)).astype(BF16)
    return high, middle, low


def dot(a, b):
    return jnp.dot(a, b, preferred_element_type=F32)


Z_GROUPS = ((0, 96), (96, 32))
X_GROUPS = ((0, 160), (160, 96))
TOGETHER = 2


def reduce_scatter(adj, rhs, bufs, sems, ids, started, before_end, on_z_rows, on_x_rows):
    sums, sent, got, z_up, z_down, x_up, x_down, tz_up, tz_down, tx_up, tx_down = bufs
    pair_sends, pair_recvs, sends, recvs = sems
    pair_id, zp_id, zm_id, xp_id, xm_id = ids
    width = rhs.shape[1]

    def pair_copy(chunk):
        return pltpu.make_async_remote_copy(
            src_ref=sent.at[chunk], dst_ref=got.at[chunk], send_sem=pair_sends.at[chunk],
            recv_sem=pair_recvs.at[chunk], device_id=pair_id, device_id_type=MESH,
        )

    def product(first, target, at):
        lhs = adj[pl.ds(first, TOGETHER)].reshape(TOGETHER * 256, 512)
        target[pl.ds(at, TOGETHER)] = dot(lhs, rhs[...]).reshape(TOGETHER, 256, width)

    def for_pair(i, carry):
        product(16 + i * TOGETHER, sent, i * TOGETHER)
        for k in range(TOGETHER):
            pair_copy(i * TOGETHER + k).start()
        return carry

    def for_own(i, carry):
        product(i * TOGETHER, sums, i * TOGETHER)
        return carry

    def run(kind, first, end):
        lax.fori_loop(first // TOGETHER, end // TOGETHER, kind, 0)

    have = set()

    def arrived(chunk):
        if chunk not in have:
            have.add(chunk)
            pair_copy(chunk).wait_recv()

    def none(offset, half):
        return []

    def z_part(group):
        first, size = Z_GROUPS[group]

        def own(dz, half):
            return sums.at[chunk_z(dz), pl.ds(half * BLK + first, size)]

        def extra(dz, half):
            arrived(chunk_z(dz))
            return [got.at[chunk_z(dz), pl.ds(half * BLK + first, size)]]

        def land(way, at, half):
            return (z_up, z_down)[way].at[at, half, pl.ds(first, size)]

        slots = pl.ds(group * 16, 16)
        return Ring(ZS, own, extra, land, zp_id, zm_id, sends.at[slots], recvs.at[slots], started)

    def x_part(group):
        first, size = X_GROUPS[group]

        def own(dx, half):
            return sums.at[chunk_x(dx, half), pl.ds(first, size)]

        def extra(dx, half):
            arrived(chunk_x(dx, half))
            return [got.at[chunk_x(dx, half), pl.ds(first, size)]]

        def land(way, at, half):
            return (x_up, x_down)[way].at[at, half, pl.ds(first, size)]

        slots = pl.ds(32 + group * 8, 8)
        return Ring(XS, own, extra, land, xp_id, xm_id, sends.at[slots], recvs.at[slots], started)

    def last_z():
        def own(dz, half):
            return sums.at[chunk_x(0, half), pl.ds(rank_of(dz, ZS // 2) * QUARTER, QUARTER)]

        def land(way, at, half):
            return (tz_up, tz_down)[way].at[at, half]

        slots = pl.ds(48, 16)
        return Ring(ZS, own, none, land, zp_id, zm_id, sends.at[slots], recvs.at[slots], started)

    def last_x():
        def own(dx, half):
            return sums.at[chunk_z(0), pl.ds(half * BLK + rank_of(dx, XS // 2) * QUARTER, QUARTER)]

        def land(way, at, half):
            return (tx_up, tx_down)[way].at[at, half]

        slots = pl.ds(64, 8)
        return Ring(XS, own, none, land, xp_id, xm_id, sends.at[slots], recvs.at[slots], started)

    z0, z1, x0, x1, tz, tx = z_part(0), z_part(1), x_part(0), x_part(1), last_z(), last_x()

    run(for_pair, 0, 4)
    run(for_own, 0, 4)
    run(for_pair, 4, 8)
    z0.late(4)
    x0.late(2)
    run(for_pair, 8, 16)
    run(for_own, 4, 8)
    z0.early(3)
    run(for_own, 8, 12)
    x0.early(1)
    z1.late(4)
    run(for_own, 12, 16)
    z0.late(3)
    z1.early(3)
    x0.late(1)
    x1.late(2)
    x1.early(1)
    z0.early(2)
    z1.late(3)
    z0.late(2)
    z1.early(2)
    z0.early(1)
    x0.finish(0)
    x0.finish(1)
    tz.late(4)
    tz.early(3)
    z0.late(1)
    x1.late(1)
    z1.late(2)
    tz.late(3)
    z1.early(1)
    tz.early(2)
    z0.finish(0)
    z0.finish(1)
    tx.late(2)
    tx.early(1)
    z1.late(1)
    tz.late(2)
    before_end()
    tx.late(1)
    x1.finish(0)
    x1.finish(1)
    tz.early(1)
    tz.late(1)
    z1.finish(0)
    z1.finish(1)
    on_z_rows(tx)
    on_x_rows(tz)

    def drain(chunk, carry):
        pair_copy(chunk).wait_send()
        return carry

    return lambda: lax.fori_loop(0, 16, drain, 0)


def net_kernel(adj, feats_ref, pack_ref, out_ref, *scratch):
    (
        feats_all, packs, feats, hidden, self_one, neigh_one, self_two, neigh_two, bias, own_part, agg_all, agg_two, slices,
        landed, *rest
    ) = scratch
    bufs_one, bufs_two, rest = rest[:11], rest[11:22], rest[22:]
    y_sends, y_recvs, sems_one, sems_two = rest[0], rest[1], rest[2:6], rest[6:10]

    feat = lax.axis_index("feat")
    x, z, core = position()

    def at(x_at, z_at, core_at, feat_at=feat):
        return feat_at, (x_at * ZS + z_at) * 2 + core_at

    pair_id = at(x, z, 1 - core)
    zp_id, zm_id = at(x, lax.rem(z + 1, ZS), core), at(x, lax.rem(z + ZS - 1, ZS), core)
    xp_id, xm_id = at(lax.rem(x + 1, XS), z, core), at(lax.rem(x + XS - 1, XS), z, core)
    y_ids = [at(x, z, core, lax.rem(feat + k, FS)) for k in range(1, FS)]
    ids = (pair_id, zp_id, zm_id, xp_id, xm_id)

    barrier = pltpu.get_barrier_semaphore()
    for other in ids + tuple(y_ids):
        pl.semaphore_signal(barrier, inc=1, device_id=other, device_id_type=MESH)
    pl.semaphore_wait(barrier, 8)

    started = []

    def to_y(kind, source, target):
        copies = []
        for k in range(1, FS):
            slot = kind * 3 + k - 1
            copies.append(
                pltpu.make_async_remote_copy(
                    src_ref=source(k), dst_ref=target, send_sem=y_sends.at[slot], recv_sem=y_recvs.at[slot],
                    device_id=y_ids[k - 1], device_id_type=MESH,
                )
            )
            copies[-1].start()
        started.extend(copies)
        return copies

    def received(copies):
        for copy in copies:
            copy.wait_recv()

    feats_rows = pl.ds(pl.multiple_of(feat * 32, 32), 32)
    feats_copies = to_y(0, lambda k: feats_ref, feats_all.at[feats_rows])
    pack_copies = to_y(1, lambda k: pack_ref, packs.at[feat])
    feats_all[feats_rows, :] = feats_ref[...]
    packs[feat] = pack_ref[...]
    received(feats_copies)
    feats[...] = feats_all[...].T.astype(BF16)

    def take_weights():
        received(pack_copies)
        low = lax.broadcasted_iota(jnp.int32, (1, BLK), 1) < 64
        for row in range(2):
            for pair in range(2):
                left = packs[2 * pair, 192 + row : 193 + row, 0:BLK]
                right = packs[2 * pair + 1, 192 + row : 193 + row, 0:BLK]
                value = jnp.where(low, left, pltpu.roll(right, 64, 1))
                bias[row : row + 1, pair * BLK : (pair + 1) * BLK] = value
        for j in range(FS):
            self_one[32 * j : 32 * (j + 1), :] = packs[j, 0:32, :].astype(BF16)
            neigh_one[32 * j : 32 * (j + 1), :] = packs[j, 32:64, :].astype(BF16)
            self_two[64 * j : 64 * (j + 1), :] = packs[j, 64:128, :].astype(BF16)
            neigh_two[64 * j : 64 * (j + 1), :] = packs[j, 128:192, :].astype(BF16)

        own_part[...] = dot(feats[...], self_one[...]) + bias[0:1, :]

    own = pl.ds(pl.multiple_of(feat * BLK, BLK), BLK)

    def own_of_two():
        own_part[0:BLK, :] = dot(hidden[own, :], self_two[...]) + bias[1:2, :]

    agg_copies = []

    def share(kind, rows, ring):
        for half in range(2):
            ring.finish(half, agg_all.at[feat, pl.ds(rows + half * QUARTER, QUARTER)])
        part = agg_all.at[feat, pl.ds(rows, 64)]
        agg_copies.extend(to_y(kind, lambda k: part, part))

    drain_one = reduce_scatter(
        adj, feats, bufs_one, sems_one, ids, started, take_weights,
        lambda ring: share(2, 64, ring), lambda ring: share(3, 0, ring),
    )
    received(agg_copies)

    def hide(j, carry):
        rows = pl.ds(pl.multiple_of(j * BLK, BLK), BLK)
        pre = own_part[rows, :]
        for part in split(agg_all[j]):
            pre = pre + dot(part, neigh_one[...])
        hidden[rows, :] = jnp.maximum(pre, 0.0).astype(BF16)
        return carry

    lax.fori_loop(0, FS, hide, 0)

    def keep(rows, ring):
        for half in range(2):
            ring.finish(half, agg_two.at[pl.ds(rows + half * QUARTER, QUARTER)])

    drain_two = reduce_scatter(
        adj, hidden, bufs_two, sems_two, ids, started, own_of_two,
        lambda ring: keep(64, ring), lambda ring: keep(0, ring),
    )

    pre = own_part[0:BLK, :]
    for part in split(agg_two[...]):
        pre = pre + dot(part, neigh_two[...])
    result = jnp.maximum(pre, 0.0)
    slices[...] = result.T.reshape(FS, 64, BLK)
    out_copies = to_y(4, lambda k: slices.at[lax.rem(feat + k, FS)], landed.at[feat])
    landed[feat] = slices[feat]
    received(out_copies)
    for j in range(FS):
        out_ref[:, j * BLK : (j + 1) * BLK] = landed[j].astype(BF16)

    drain_one()
    drain_two()
    for copy in started:
        copy.wait_send()


def layer_buffers(width):
    shapes = [(16, 256, width)] * 3
    shapes += [(4, 2, 128, width)] * 2 + [(2, 2, 256, width)] * 2 + [(4, 2, 32, width)] * 2 + [(2, 2, 32, width)] * 2
    return [pltpu.VMEM(shape, F32) for shape in shapes]


def net(adj, feats, pack):
    vmem = pl.BlockSpec(memory_space=pltpu.VMEM)
    dma = pltpu.SemaphoreType.DMA
    return pl.pallas_call(
        net_kernel,
        out_shape=jax.ShapeDtypeStruct((64, 512), BF16),
        in_specs=[vmem] * 3,
        out_specs=vmem,
        scratch_shapes=[
            pltpu.VMEM((128, 512), F32),
            pltpu.VMEM((FS, PACK_ROWS, 256), F32),
            pltpu.VMEM((512, 128), BF16),
            pltpu.VMEM((512, 256), BF16),
            pltpu.VMEM((128, 256), BF16),
            pltpu.VMEM((128, 256), BF16),
            pltpu.VMEM((256, 256), BF16),
            pltpu.VMEM((256, 256), BF16),
            pltpu.VMEM((8, 256), F32),
            pltpu.VMEM((512, 256), F32),
            pltpu.VMEM((FS, 128, 128), F32),
            pltpu.VMEM((128, 256), F32),
            pltpu.VMEM((FS, 64, 128), F32),
            pltpu.VMEM((FS, 64, 128), F32),
        ]
        + layer_buffers(128)
        + layer_buffers(256)
        + [dma((15,)), dma((15,))]
        + [dma((16,)), dma((16,)), dma((72,)), dma((72,))] * 2,
        compiler_params=pltpu.CompilerParams(
            collective_id=0, has_side_effects=True, vmem_limit_bytes=36 << 20
        ),
    )(*[pltpu.with_memory_space_constraint(array, pltpu.VMEM) for array in (adj, feats, pack)])


def on_device(
    feats, tile_src, tile_dst, tile_val, tile_count, self_one, neigh_one, bias_one, self_two, neigh_two, bias_two
):
    adj, columns, pack = build(
        tile_src, tile_dst, tile_count, tile_val, feats.T, self_one, neigh_one, bias_one.reshape(1, 64), self_two,
        neigh_two, bias_two.reshape(1, 64),
    )
    return net(adj, columns, pack).T


def solution(mesh):
    placed = (
        P("dom", "feat"),
        P("dom"),
        P("dom"),
        P("dom", None, None),
        P("dom"),
        P("feat", None),
        P("feat", None),
        P("feat"),
        P("feat", None),
        P("feat", None),
        P("feat"),
    )
    return jax.shard_map(
        on_device, mesh=mesh, in_specs=placed, out_specs=P("dom", "feat"), check_vma=False
    )
```

time: 482 us -> 91.5 us (0.19)
  waiting for transfers between devices: 366 us -> 0 us
  Pallas kernels: 0 us -> 90.1 us
  local copies, waits for them, and re-layouts: 55.4 us -> 0.63 us
  matrix products: 41.5 us -> 0 us
  between operations: 13.9 us -> 0.67 us
    reduce_scatter x3 -> x0, waiting for transfers between devices: 319 us -> none  [the longest x1 150 us: on_device(): lax.psum_scatter(packed_term(messages_two, tile_dst, live, node_rows // f...]
    pallas_call x0 -> x2, Pallas kernels: none -> 90.1 us  [the longest x1 84.7 us: net(): pl.pallas_call(net_kernel, out_shape=jax.ShapeDtypeStruct((64, 512), BF16...]
    psum x1 -> x0, waiting for transfers between devices: 47.4 us -> none  [on_device(): summed = lax.psum(partial_one, 'feat')]
    dot_general x8 -> x0, matrix products: 41.5 us -> none  [the longest x2 20.3 us: route_rows(): jnp.einsum('bt,tic->bic', routing, messages, precision=lax.Precision.HIGH...]
    another operation x2 -> x0, local copies, waits for them, and re-layouts: 25.8 us -> none  [packed_term(): return node_term.reshape(count, width * factor)]
    dot_general x2 -> x0, local copies, waits for them, and re-layouts: 22.9 us -> none  [route_rows(): jnp.einsum('bt,tic->bic', routing, messages, precision=lax.Precision.HIGH...]
  transfers between devices with their start and end apart: 4 -> 0, of which waited for: 4 -> 0; matrix products, arithmetic and copies ran while one was open for 0% -> 0% of each run, Pallas kernels for 0% -> 0%
where the time goes in v1:
time: 91.5 us; the launch traced here: 91.4 us
  Pallas kernels  90.1 us (98%)
    pallas_call x1, Pallas kernels, net(): pl.pallas_call(net_kernel, out_shape=jax.ShapeDtypeStruct((64, 512), BF16...  84.7 us
    pallas_call x1, Pallas kernels, build(): pl.pallas_call(build_kernel, out_shape=(pltpu.VMEM((32, 256, 512), BF16),...  5.44 us

profile of v1, /device:TPU:2, one launch (start us, length us, event | category | flops | bytes accessed | tf_op | source)
XLA Modules:
  0.0 91.4 jit_solution(1896476935400341451)
XLA Ops:
  0.7 5.4 %shard_map.109 = (bf16[32,256,512]{2,1,0:T(8,128)(2,1)S(1)}, f32[32,512]{1,0:T(8,128)S(1)}, f32[200,256]{1,0:T(8,128)S(1)}) custom-call(s32[1]{0:T(128)S(6)} %copy.13.count_ref, s32[256]{0:T(256)} %src_ref.1, s32[256]{0:T(256)} %dst_ref.1, bf16[256,128,128]{2,1,0:T(8,128)(2,1)} %tiles_ref.1, bf16[32,512]{1,0:T(8,128)(2,1)} %bitcast.5, ...), custom_call_target="tpu_custom_call" | custom-call | tf_op jit(solution)/shard_map/pallas_call | solution.py:163
  6.1 84.7 %shard_map.110 = bf16[64,512]{1,0:T(8,128)(2,1)S(1)} custom-call(bf16[32,256,512]{2,1,0:T(8,128)(2,1)S(1)} %get-tuple-element.8.adj, f32[32,512]{1,0:T(8,128)S(1)} %get-tuple-element.9.feats_ref, f32[200,256]{1,0:T(8,128)S(1)} %get-tuple-element.10.pack_ref), custom_call_target="tpu_custom_call" | custom-call | tf_op jit(solution)/shard_map/pallas_call | solution.py:555
  90.8 0.6 copy.14

commit v2 on v1

--- a/solution.py
+++ b/solution.py
@@ -103,11 +103,11 @@
     feats_out[...] = feats[...].astype(F32)
     pack_out[0:32, :] = self_one[...].astype(F32)
     pack_out[32:64, :] = neigh_one[...].astype(F32)
-    pack_out[64:128, :] = self_two[...].astype(F32)
-    pack_out[128:192, :] = neigh_two[...].astype(F32)
-    pack_out[192:200, :] = jnp.zeros((8, 256), F32)
-    pack_out[192:193, 0:64] = bias_one[...]
-    pack_out[193:194, 0:64] = bias_two[...]
+    pack_out[64:72, :] = jnp.zeros((8, 256), F32)
+    pack_out[64:65, 0:64] = bias_one[...]
+    pack_out[65:66, 0:64] = bias_two[...]
+    pack_out[72:136, :] = self_two[...].astype(F32)
+    pack_out[136:200, :] = neigh_two[...].astype(F32)
 
     def put(cell, value):
         source = cell & 3
@@ -129,23 +129,18 @@
         t = order[i]
         cell = cells[i]
         before = earlier[t]
-
-        @pl.when(last[cell] == t)
+        put(cell, tiles[t])
+
+        @pl.when(jnp.logical_and(before >= 0, last[cell] == t))
         def _():
-            @pl.when(before < 0)
-            def _():
-                put(cell, tiles[t])
-
-            @pl.when(before >= 0)
-            def _():
-                total[...] = tiles[t].astype(F32)
-
-                def more(at):
-                    total[...] += tiles[at].astype(F32)
-                    return earlier[at]
-
-                lax.while_loop(lambda at: at >= 0, more, before)
-                put(cell, total[...].astype(BF16))
+            total[...] = tiles[t].astype(F32)
+
+            def more(at):
+                total[...] += tiles[at].astype(F32)
+                return earlier[at]
+
+            lax.while_loop(lambda at: at >= 0, more, before)
+            put(cell, total[...].astype(BF16))
 
         return carry
 
@@ -252,6 +247,36 @@
         add_up(mine if into is None else into, terms)
 
 
+class Direct:
+    def __init__(self, n, own, landing, target_ids, sends, recvs, started):
+        self.n, self.own, self.landing, self.ids = n, own, landing, target_ids
+        self.sends, self.recvs, self.started = sends, recvs, started
+
+    def copy(self, offset, half):
+        slot = (offset - 1) * 2 + half
+        return pltpu.make_async_remote_copy(
+            src_ref=self.own(offset, half),
+            dst_ref=self.landing.at[offset - 1, half],
+            send_sem=self.sends.at[slot],
+            recv_sem=self.recvs.at[slot],
+            device_id=self.ids[offset - 1],
+            device_id_type=MESH,
+        )
+
+    def send(self, offset):
+        for half in range(2):
+            copy = self.copy(offset, half)
+            copy.start()
+            self.started.append(copy)
+
+    def finish(self, half, into):
+        terms = [self.own(0, half)]
+        for offset in range(1, self.n):
+            self.copy(offset, half).wait_recv()
+            terms.append(self.landing.at[offset - 1, half])
+        add_up(into, terms)
+
+
 def split(value):
     high = value.astype(BF16)
     rest = value - high.astype(F32)
@@ -269,10 +294,11 @@
 TOGETHER = 2
 
 
-def reduce_scatter(adj, rhs, bufs, sems, ids, started, before_end, on_z_rows, on_x_rows):
-    sums, sent, got, z_up, z_down, x_up, x_down, tz_up, tz_down, tx_up, tx_down = bufs
+def reduce_scatter(adj, rhs, bufs, sems, ids, started, after_start, before_end, on_z_rows, on_x_rows):
+    sums, sent, got, z_up, z_down, x_up, x_down, tz_up, tz_down, tx_in = bufs
     pair_sends, pair_recvs, sends, recvs = sems
-    pair_id, zp_id, zm_id, xp_id, xm_id = ids
+    pair_id, zp_id, zm_id, *x_ids = ids
+    xp_id, xm_id = x_ids[0], x_ids[2]
     width = rhs.shape[1]
 
     def pair_copy(chunk):
@@ -354,31 +380,28 @@
         def own(dx, half):
             return sums.at[chunk_z(0), pl.ds(half * BLK + rank_of(dx, XS // 2) * QUARTER, QUARTER)]
 
-        def land(way, at, half):
-            return (tx_up, tx_down)[way].at[at, half]
-
-        slots = pl.ds(64, 8)
-        return Ring(XS, own, none, land, xp_id, xm_id, sends.at[slots], recvs.at[slots], started)
+        return Direct(XS, own, tx_in, x_ids, sends.at[pl.ds(64, 6)], recvs.at[pl.ds(64, 6)], started)
 
     z0, z1, x0, x1, tz, tx = z_part(0), z_part(1), x_part(0), x_part(1), last_z(), last_x()
 
-    run(for_pair, 0, 4)
+    run(for_pair, 0, 8)
     run(for_own, 0, 4)
-    run(for_pair, 4, 8)
     z0.late(4)
     x0.late(2)
-    run(for_pair, 8, 16)
+    run(for_pair, 8, 12)
     run(for_own, 4, 8)
     z0.early(3)
+    z1.late(4)
+    z1.early(3)
     run(for_own, 8, 12)
     x0.early(1)
-    z1.late(4)
+    run(for_pair, 12, 16)
     run(for_own, 12, 16)
     z0.late(3)
-    z1.early(3)
     x0.late(1)
     x1.late(2)
     x1.early(1)
+    after_start()
     z0.early(2)
     z1.late(3)
     z0.late(2)
@@ -396,12 +419,11 @@
     tz.early(2)
     z0.finish(0)
     z0.finish(1)
-    tx.late(2)
-    tx.early(1)
+    for dx in (2, 1, 3):
+        tx.send(dx)
     z1.late(1)
     tz.late(2)
     before_end()
-    tx.late(1)
     x1.finish(0)
     x1.finish(1)
     tz.early(1)
@@ -423,7 +445,7 @@
         feats_all, packs, feats, hidden, self_one, neigh_one, self_two, neigh_two, bias, own_part, agg_all, agg_two, slices,
         landed, *rest
     ) = scratch
-    bufs_one, bufs_two, rest = rest[:11], rest[11:22], rest[22:]
+    bufs_one, bufs_two, rest = rest[:10], rest[10:20], rest[20:]
     y_sends, y_recvs, sems_one, sems_two = rest[0], rest[1], rest[2:6], rest[6:10]
 
     feat = lax.axis_index("feat")
@@ -434,14 +456,14 @@
 
     pair_id = at(x, z, 1 - core)
     zp_id, zm_id = at(x, lax.rem(z + 1, ZS), core), at(x, lax.rem(z + ZS - 1, ZS), core)
-    xp_id, xm_id = at(lax.rem(x + 1, XS), z, core), at(lax.rem(x + XS - 1, XS), z, core)
+    x_ids = [at(lax.rem(x + k, XS), z, core) for k in range(1, XS)]
     y_ids = [at(x, z, core, lax.rem(feat + k, FS)) for k in range(1, FS)]
-    ids = (pair_id, zp_id, zm_id, xp_id, xm_id)
+    ids = (pair_id, zp_id, zm_id, *x_ids)
 
     barrier = pltpu.get_barrier_semaphore()
     for other in ids + tuple(y_ids):
         pl.semaphore_signal(barrier, inc=1, device_id=other, device_id_type=MESH)
-    pl.semaphore_wait(barrier, 8)
+    pl.semaphore_wait(barrier, 9)
 
     started = []
 
@@ -456,7 +478,8 @@
                 )
             )
             copies[-1].start()
-        started.extend(copies)
+        if kind != 4:
+            started.extend(copies)
         return copies
 
     def received(copies):
@@ -465,32 +488,39 @@
 
     feats_rows = pl.ds(pl.multiple_of(feat * 32, 32), 32)
     feats_copies = to_y(0, lambda k: feats_ref, feats_all.at[feats_rows])
-    pack_copies = to_y(1, lambda k: pack_ref, packs.at[feat])
     feats_all[feats_rows, :] = feats_ref[...]
     packs[feat] = pack_ref[...]
     received(feats_copies)
     feats[...] = feats_all[...].T.astype(BF16)
 
+    pack_copies = []
+
+    def send_pack(kind, first, size):
+        rows = pl.ds(first, size)
+        pack_copies.append(to_y(kind, lambda k: pack_ref.at[rows], packs.at[feat, rows]))
+
     def take_weights():
-        received(pack_copies)
+        received(pack_copies[0])
         low = lax.broadcasted_iota(jnp.int32, (1, BLK), 1) < 64
         for row in range(2):
             for pair in range(2):
-                left = packs[2 * pair, 192 + row : 193 + row, 0:BLK]
-                right = packs[2 * pair + 1, 192 + row : 193 + row, 0:BLK]
+                left = packs[2 * pair, 64 + row : 65 + row, 0:BLK]
+                right = packs[2 * pair + 1, 64 + row : 65 + row, 0:BLK]
                 value = jnp.where(low, left, pltpu.roll(right, 64, 1))
                 bias[row : row + 1, pair * BLK : (pair + 1) * BLK] = value
         for j in range(FS):
             self_one[32 * j : 32 * (j + 1), :] = packs[j, 0:32, :].astype(BF16)
             neigh_one[32 * j : 32 * (j + 1), :] = packs[j, 32:64, :].astype(BF16)
-            self_two[64 * j : 64 * (j + 1), :] = packs[j, 64:128, :].astype(BF16)
-            neigh_two[64 * j : 64 * (j + 1), :] = packs[j, 128:192, :].astype(BF16)
 
         own_part[...] = dot(feats[...], self_one[...]) + bias[0:1, :]
 
     own = pl.ds(pl.multiple_of(feat * BLK, BLK), BLK)
 
     def own_of_two():
+        received(pack_copies[1])
+        for j in range(FS):
+            self_two[64 * j : 64 * (j + 1), :] = packs[j, 72:136, :].astype(BF16)
+            neigh_two[64 * j : 64 * (j + 1), :] = packs[j, 136:200, :].astype(BF16)
         own_part[0:BLK, :] = dot(hidden[own, :], self_two[...]) + bias[1:2, :]
 
     agg_copies = []
@@ -502,7 +532,7 @@
         agg_copies.extend(to_y(kind, lambda k: part, part))
 
     drain_one = reduce_scatter(
-        adj, feats, bufs_one, sems_one, ids, started, take_weights,
+        adj, feats, bufs_one, sems_one, ids, started, lambda: send_pack(1, 0, 72), take_weights,
         lambda ring: share(2, 64, ring), lambda ring: share(3, 0, ring),
     )
     received(agg_copies)
@@ -522,7 +552,7 @@
             ring.finish(half, agg_two.at[pl.ds(rows + half * QUARTER, QUARTER)])
 
     drain_two = reduce_scatter(
-        adj, hidden, bufs_two, sems_two, ids, started, own_of_two,
+        adj, hidden, bufs_two, sems_two, ids, started, lambda: send_pack(5, 72, 128), own_of_two,
         lambda ring: keep(64, ring), lambda ring: keep(0, ring),
     )
 
@@ -533,19 +563,21 @@
     slices[...] = result.T.reshape(FS, 64, BLK)
     out_copies = to_y(4, lambda k: slices.at[lax.rem(feat + k, FS)], landed.at[feat])
     landed[feat] = slices[feat]
-    received(out_copies)
-    for j in range(FS):
-        out_ref[:, j * BLK : (j + 1) * BLK] = landed[j].astype(BF16)
-
     drain_one()
     drain_two()
     for copy in started:
         copy.wait_send()
+    received(out_copies)
+    for j in range(FS):
+        out_ref[:, j * BLK : (j + 1) * BLK] = landed[j].astype(BF16)
+
+    for copy in out_copies:
+        copy.wait_send()
 
 
 def layer_buffers(width):
     shapes = [(16, 256, width)] * 3
-    shapes += [(4, 2, 128, width)] * 2 + [(2, 2, 256, width)] * 2 + [(4, 2, 32, width)] * 2 + [(2, 2, 32, width)] * 2
+    shapes += [(4, 2, 128, width)] * 2 + [(2, 2, 256, width)] * 2 + [(4, 2, 32, width)] * 2 + [(3, 2, 32, width)]
     return [pltpu.VMEM(shape, F32) for shape in shapes]
 
 
@@ -575,7 +607,7 @@
         ]
         + layer_buffers(128)
         + layer_buffers(256)
-        + [dma((15,)), dma((15,))]
+        + [dma((18,)), dma((18,))]
         + [dma((16,)), dma((16,)), dma((72,)), dma((72,))] * 2,
         compiler_params=pltpu.CompilerParams(
             collective_id=0, has_side_effects=True, vmem_limit_bytes=36 << 20

time: 91.5 us -> 87.5 us (0.956); the launches traced: 91.4 us -> 86.5 us
  Pallas kernels: 90.1 us -> 85.2 us
    pallas_call x1, Pallas kernels: 84.7 us -> 80.2 us  [net(): pl.pallas_call(net_kernel, out_shape=jax.ShapeDtypeStruct((64, 512), BF16...]
where the time goes in v2:
time: 87.5 us; the launch traced here: 86.5 us
  Pallas kernels  85.2 us (97%)
    pallas_call x1, Pallas kernels, net(): pl.pallas_call(net_kernel, out_shape=jax.ShapeDtypeStruct((64, 512), BF16...  80.2 us
    pallas_call x1, Pallas kernels, build(): pl.pallas_call(build_kernel, out_shape=(pltpu.VMEM((32, 256, 512), BF16),...  5 us

profile of v2, /device:TPU:2, one launch (start us, length us, event | category | flops | bytes accessed | tf_op | source)
XLA Modules:
  0.0 86.5 jit_solution(9899421599497357829)
XLA Ops:
  0.7 5.0 %shard_map.109 = (bf16[32,256,512]{2,1,0:T(8,128)(2,1)S(1)}, f32[32,512]{1,0:T(8,128)S(1)}, f32[200,256]{1,0:T(8,128)S(1)}) custom-call(s32[1]{0:T(128)S(6)} %copy.13.count_ref, s32[256]{0:T(256)} %src_ref.1, s32[256]{0:T(256)} %dst_ref.1, bf16[256,128,128]{2,1,0:T(8,128)(2,1)} %tiles_ref.1, bf16[32,512]{1,0:T(8,128)(2,1)} %bitcast.5, ...), custom_call_target="tpu_custom_call" | custom-call | tf_op jit(solution)/shard_map/pallas_call | solution.py:158
  5.7 80.2 %shard_map.110 = bf16[64,512]{1,0:T(8,128)(2,1)S(1)} custom-call(bf16[32,256,512]{2,1,0:T(8,128)(2,1)S(1)} %get-tuple-element.8.adj, f32[32,512]{1,0:T(8,128)S(1)} %get-tuple-element.9.feats_ref, f32[200,256]{1,0:T(8,128)S(1)} %get-tuple-element.10.pack_ref), custom_call_target="tpu_custom_call" | custom-call | tf_op jit(solution)/shard_map/pallas_call | solution.py:587
  85.8 0.6 copy.14

commit v3 on v2

--- a/solution.py
+++ b/solution.py
@@ -290,7 +290,7 @@
 
 
 Z_GROUPS = ((0, 96), (96, 32))
-X_GROUPS = ((0, 160), (160, 96))
+X_GROUPS = ((0, 96), (96, 64), (160, 96))
 TOGETHER = 2
 
 
@@ -373,16 +373,16 @@
         def land(way, at, half):
             return (tz_up, tz_down)[way].at[at, half]
 
-        slots = pl.ds(48, 16)
+        slots = pl.ds(56, 16)
         return Ring(ZS, own, none, land, zp_id, zm_id, sends.at[slots], recvs.at[slots], started)
 
     def last_x():
         def own(dx, half):
             return sums.at[chunk_z(0), pl.ds(half * BLK + rank_of(dx, XS // 2) * QUARTER, QUARTER)]
 
-        return Direct(XS, own, tx_in, x_ids, sends.at[pl.ds(64, 6)], recvs.at[pl.ds(64, 6)], started)
-
-    z0, z1, x0, x1, tz, tx = z_part(0), z_part(1), x_part(0), x_part(1), last_z(), last_x()
+        return Direct(XS, own, tx_in, x_ids, sends.at[pl.ds(72, 6)], recvs.at[pl.ds(72, 6)], started)
+
+    z0, z1, x0, x1, x2, tz, tx = z_part(0), z_part(1), x_part(0), x_part(1), x_part(2), last_z(), last_x()
 
     run(for_pair, 0, 8)
     run(for_own, 0, 4)
@@ -404,28 +404,33 @@
     after_start()
     z0.early(2)
     z1.late(3)
-    z0.late(2)
-    z1.early(2)
-    z0.early(1)
     x0.finish(0)
     x0.finish(1)
     tz.late(4)
     tz.early(3)
+    z0.late(2)
+    x1.late(1)
+    x2.late(2)
+    x2.early(1)
+    z1.early(2)
+    z0.early(1)
+    tz.late(3)
+    x1.finish(0)
+    x1.finish(1)
+    tz.early(2)
     z0.late(1)
-    x1.late(1)
     z1.late(2)
-    tz.late(3)
+    x2.late(1)
+    tz.late(2)
     z1.early(1)
-    tz.early(2)
     z0.finish(0)
     z0.finish(1)
     for dx in (2, 1, 3):
         tx.send(dx)
     z1.late(1)
-    tz.late(2)
     before_end()
-    x1.finish(0)
-    x1.finish(1)
+    x2.finish(0)
+    x2.finish(1)
     tz.early(1)
     tz.late(1)
     z1.finish(0)
@@ -537,15 +542,10 @@
     )
     received(agg_copies)
 
-    def hide(j, carry):
-        rows = pl.ds(pl.multiple_of(j * BLK, BLK), BLK)
-        pre = own_part[rows, :]
-        for part in split(agg_all[j]):
-            pre = pre + dot(part, neigh_one[...])
-        hidden[rows, :] = jnp.maximum(pre, 0.0).astype(BF16)
-        return carry
-
-    lax.fori_loop(0, FS, hide, 0)
+    pre = own_part[...]
+    for part in split(agg_all[...].reshape(FS * BLK, BLK)):
+        pre = pre + dot(part, neigh_one[...])
+    hidden[...] = jnp.maximum(pre, 0.0).astype(BF16)
 
     def keep(rows, ring):
         for half in range(2):
@@ -608,7 +608,7 @@
         + layer_buffers(128)
         + layer_buffers(256)
         + [dma((18,)), dma((18,))]
-        + [dma((16,)), dma((16,)), dma((72,)), dma((72,))] * 2,
+        + [dma((16,)), dma((16,)), dma((80,)), dma((80,))] * 2,
         compiler_params=pltpu.CompilerParams(
             collective_id=0, has_side_effects=True, vmem_limit_bytes=36 << 20
         ),

time: 87.5 us -> 84.4 us (0.965)
  Pallas kernels: 85.2 us -> 82.9 us
    pallas_call x1, Pallas kernels: 80.2 us -> 78.5 us  [net(): pl.pallas_call(net_kernel, out_shape=jax.ShapeDtypeStruct((64, 512), BF16...]
where the time goes in v3:
time: 84.4 us; the launch traced here: 84.2 us
  Pallas kernels  82.9 us (98%)
    pallas_call x1, Pallas kernels, net(): pl.pallas_call(net_kernel, out_shape=jax.ShapeDtypeStruct((64, 512), BF16...  78.5 us
    pallas_call x1, Pallas kernels, build(): pl.pallas_call(build_kernel, out_shape=(pltpu.VMEM((32, 256, 512), BF16),...  4.33 us

profile of v3, /device:TPU:2, one launch (start us, length us, event | category | flops | bytes accessed | tf_op | source)
XLA Modules:
  0.0 84.2 jit_solution(4103440715359363159)
XLA Ops:
  0.7 4.3 %shard_map.109 = (bf16[32,256,512]{2,1,0:T(8,128)(2,1)S(1)}, f32[32,512]{1,0:T(8,128)S(1)}, f32[200,256]{1,0:T(8,128)S(1)}) custom-call(s32[1]{0:T(128)S(6)} %copy.13.count_ref, s32[256]{0:T(256)} %src_ref.1, s32[256]{0:T(256)} %dst_ref.1, bf16[256,128,128]{2,1,0:T(8,128)(2,1)} %tiles_ref.1, bf16[32,512]{1,0:T(8,128)(2,1)} %bitcast.5, ...), custom_call_target="tpu_custom_call" | custom-call | tf_op jit(solution)/shard_map/pallas_call | solution.py:158
  5.0 78.5 %shard_map.110 = bf16[64,512]{1,0:T(8,128)(2,1)S(1)} custom-call(bf16[32,256,512]{2,1,0:T(8,128)(2,1)S(1)} %get-tuple-element.8.adj, f32[32,512]{1,0:T(8,128)S(1)} %get-tuple-element.9.feats_ref, f32[200,256]{1,0:T(8,128)S(1)} %get-tuple-element.10.pack_ref), custom_call_target="tpu_custom_call" | custom-call | tf_op jit(solution)/shard_map/pallas_call | solution.py:587
  83.5 0.6 copy.14

commit v4 on v3

--- a/solution.py
+++ b/solution.py
@@ -415,14 +415,14 @@
     z1.early(2)
     z0.early(1)
     tz.late(3)
+    z0.late(1)
     x1.finish(0)
     x1.finish(1)
     tz.early(2)
-    z0.late(1)
     z1.late(2)
     x2.late(1)
+    z1.early(1)
     tz.late(2)
-    z1.early(1)
     z0.finish(0)
     z0.finish(1)
     for dx in (2, 1, 3):

time: 84.4 us -> 84.6 us (level); the launches traced: 84.2 us -> 83.5 us
    pallas_call x1, Pallas kernels: 78.5 us -> 77.1 us  [net(): pl.pallas_call(net_kernel, out_shape=jax.ShapeDtypeStruct((64, 512), BF16...]
where the time goes in v4:
time: 84.6 us; the launch traced here: 83.5 us
  Pallas kernels  82.2 us (97%)
    pallas_call x1, Pallas kernels, net(): pl.pallas_call(net_kernel, out_shape=jax.ShapeDtypeStruct((64, 512), BF16...  77.1 us
    pallas_call x1, Pallas kernels, build(): pl.pallas_call(build_kernel, out_shape=(pltpu.VMEM((32, 256, 512), BF16),...  5.1 us

profile of v4, /device:TPU:2, one launch (start us, length us, event | category | flops | bytes accessed | tf_op | source)
XLA Modules:
  0.0 83.5 jit_solution(5669643877732782172)
XLA Ops:
  0.7 5.1 %shard_map.109 = (bf16[32,256,512]{2,1,0:T(8,128)(2,1)S(1)}, f32[32,512]{1,0:T(8,128)S(1)}, f32[200,256]{1,0:T(8,128)S(1)}) custom-call(s32[1]{0:T(128)S(6)} %copy.13.count_ref, s32[256]{0:T(256)} %src_ref.1, s32[256]{0:T(256)} %dst_ref.1, bf16[256,128,128]{2,1,0:T(8,128)(2,1)} %tiles_ref.1, bf16[32,512]{1,0:T(8,128)(2,1)} %bitcast.5, ...), custom_call_target="tpu_custom_call" | custom-call | tf_op jit(solution)/shard_map/pallas_call | solution.py:158
  5.8 77.1 %shard_map.110 = bf16[64,512]{1,0:T(8,128)(2,1)S(1)} custom-call(bf16[32,256,512]{2,1,0:T(8,128)(2,1)S(1)} %get-tuple-element.8.adj, f32[32,512]{1,0:T(8,128)S(1)} %get-tuple-element.9.feats_ref, f32[200,256]{1,0:T(8,128)S(1)} %get-tuple-element.10.pack_ref), custom_call_target="tpu_custom_call" | custom-call | tf_op jit(solution)/shard_map/pallas_call | solution.py:587
  82.9 0.6 copy.14
